TPU v7x, 128 devices: a whole 4x4x4 slice. The times are simulated.
128 devices in a mesh: gx: 4 (over y_hi, core), gy: 4 (over z), ta: 8 (over x, y_lo).
Axes of the slice: x: 4, y: 4 (y_hi: 2, y_lo: 2; y = y_hi * 2 + y_lo), z: 4, core: 2. Of those that a mesh axis runs over, the one named last changes fastest.
Arguments:
- features: bfloat16 [32, 16, 16, 128, 256], P('ta', 'gx', 'gy'), may hold values from -6 to 6
- neighbours: int32 [16, 16, 4], P('gx', 'gy'), may hold values from 0 to 8, as said below
- adjacency: int32 [16, 16, 4, 128, 128], P('gx', 'gy'), may hold values 0 or 1
- w_space: bfloat16 [256, 256], replicated, may hold values from -0.375 to 0.375
- w_time: bfloat16 [3, 256, 256], replicated, may hold values from -0.21875 to 0.21875
- cotangent: bfloat16 [32, 16, 16, 128, 256], P('ta', 'gx', 'gy'), may hold values from -6 to 6
Outputs:
- updated: bfloat16 [32, 16, 16, 128, 256], P('ta', 'gx', 'gy')
- grad_space: float32 [256, 256], replicated
- grad_time: float32 [3, 256, 256], replicated
Inputs may be any that keep to these rules, and one draw needn't show every extreme that they name: `neighbours`: the 4 codes of a tile are distinct; code c names the tile c // 3 - 1 tiles away along x and c % 3 - 1 tiles away along y, periodically.
All inputs are finite; a program needn't handle non-finite values. No bound on the sum of `adjacency` on one device may be relied on, other than what follows from the above.
Results may differ from a plain program's by a relative error of at most 0.0068.
Values may be sent and summed in bfloat16 or wider, within the bound.
No kernel may reach another device: no remote copies, remote signals or barrier semaphores. Data moves between devices by JAX's collectives and lax.ppermute only.
A program may use at most 128 MiB of HBM per device.

v0:
```python
import math
import jax
import jax.numpy as jnp
from jax import lax
from jax.sharding import PartitionSpec as P


def with_halo(block, sides, width):
    for axis, dim in sides:
        count = lax.axis_size(axis)
        forward = [(i, i + 1) for i in range(count - 1)]
        forward.append((count - 1, 0))
        backward = [(target, source) for source, target in forward]
        low = lax.ppermute(
            lax.slice_in_dim(block, block.shape[dim] - width, None, axis=dim), axis, forward
        )
        high = lax.ppermute(lax.slice_in_dim(block, 0, width, axis=dim), axis, backward)
        block = jnp.concatenate([low, block, high], axis=dim)
    return block


def from_behind(block, axis, distance):
    devices = range(lax.axis_size(axis))
    route = [(i - distance, i) for i in devices if i - distance in devices]
    return lax.ppermute(block, axis, route)


def shards(features, neighbours, adjacency, w_space, w_time, cotangent):
    frames, tiles_x, tiles_y, lipids, feat_width = features.shape
    tap_count = w_time.shape[0]
    slot_count = neighbours.shape[2]
    behind = tap_count - 1
    tile_count = tiles_x * tiles_y
    row_count = tile_count * lipids
    extended = with_halo(features, (("gx", 1), ("gy", 2)), 1)
    flat_tiles = extended.reshape(frames, (tiles_x + 2) * (tiles_y + 2), lipids, feat_width)
    along_x = jnp.arange(tiles_x, dtype=jnp.int32)[:, None]
    along_y = jnp.arange(tiles_y, dtype=jnp.int32)[None, :]
    summed = jnp.zeros((frames, tile_count, lipids, feat_width), jnp.float32)
    for slot_pos in range(slot_count):
        offset_code = neighbours[:, :, slot_pos]
        source_index = (
            (along_x + offset_code // 3) * (tiles_y + 2) + along_y + offset_code % 3
        ).reshape(-1)
        picked = jnp.take(flat_tiles, source_index, axis=1)
        lipid_mask = (
            adjacency[:, :, slot_pos].reshape(tile_count, lipids, lipids).astype(jnp.bfloat16)
        )
        summed = summed + jnp.einsum(
            "tij,ftjc->ftic", lipid_mask, picked, preferred_element_type=jnp.float32
        )
    aggregate = (0.18 * summed).astype(jnp.bfloat16).reshape(frames * row_count, feat_width)
    projected = jnp.dot(aggregate, w_space, preferred_element_type=jnp.float32).astype(jnp.bfloat16)
    projected = projected.reshape(frames, row_count, feat_width)
    mixed = jnp.zeros((frames, row_count, feat_width), jnp.float32)
    blank = jnp.zeros((behind, row_count, feat_width), jnp.bfloat16)
    padded = jnp.concatenate([blank, projected, blank], axis=0)
    for offset in range(tap_count):
        window = padded[behind - offset : behind - offset + frames].reshape(-1, feat_width)
        mixed = mixed + jnp.dot(window, w_time[offset], preferred_element_type=jnp.float32).reshape(
            frames, row_count, feat_width
        )
    partial_terms = jnp.zeros((behind, row_count, feat_width), jnp.float32)
    for offset in range(1, tap_count):
        window = padded[behind + frames - offset : behind + frames - offset + behind].reshape(
            -1, feat_width
        )
        partial_terms = partial_terms + jnp.dot(
            window, w_time[offset], preferred_element_type=jnp.float32
        ).reshape(behind, row_count, feat_width)
    carried = from_behind(partial_terms, "ta", 1)
    mixed = mixed + jnp.concatenate(
        [carried, jnp.zeros((frames - behind, row_count, feat_width), jnp.float32)], axis=0
    )
    sigmoid_z = jax.nn.sigmoid(mixed)
    own = features.reshape(frames, row_count, feat_width).astype(jnp.float32)
    updated = (own + mixed * sigmoid_z).astype(jnp.bfloat16).reshape(features.shape)
    grad_in = cotangent.reshape(frames, row_count, feat_width).astype(jnp.float32)
    grad_mixed = (grad_in * sigmoid_z * (1.0 + mixed * (1.0 - sigmoid_z))).astype(jnp.bfloat16)
    next_grads = from_behind(grad_mixed[:behind], "ta", -1)
    joined = jnp.concatenate([grad_mixed, next_grads], axis=0)
    proj_rows = projected.reshape(-1, feat_width)
    contract = (((0,), (0,)), ((), ()))
    row_scale = 1.0 / math.sqrt(
        frames * row_count * lax.axis_size("gx") * lax.axis_size("gy") * lax.axis_size("ta")
    )
    parts = []
    for offset in range(tap_count):
        later = joined[offset : offset + frames].reshape(-1, feat_width)
        parts.append(
            lax.dot_general(proj_rows, later, contract, preferred_element_type=jnp.float32)
        )
    grad_proj = jnp.zeros((frames * row_count, feat_width), jnp.float32)
    for offset in range(tap_count):
        later = joined[offset : offset + frames].reshape(-1, feat_width)
        grad_proj = grad_proj + jnp.dot(later, w_time[offset].T, preferred_element_type=jnp.float32)
    grad_proj = grad_proj.astype(jnp.bfloat16)
    grad_space, grad_time = lax.psum(
        (
            lax.dot_general(aggregate, grad_proj, contract, preferred_element_type=jnp.float32),
            jnp.stack(parts),
        ),
        ("gx", "gy", "ta"),
    )
    return (updated, grad_space * row_scale, grad_time * row_scale)


def solution(mesh):
    in_specs = (
        P("ta", "gx", "gy", None, None),
        P("gx", "gy", None),
        P("gx", "gy", None, None, None),
        P(),
        P(),
        P("ta", "gx", "gy", None, None),
    )
    out_specs = (P("ta", "gx", "gy", None, None), P(), P())
    return jax.shard_map(shards, mesh=mesh, in_specs=in_specs, out_specs=out_specs, check_vma=False)
```

profile of v0, /device:TPU:1, one launch (start us, length us, event | category | flops | bytes accessed | tf_op | source)
XLA Modules:
  0.0 478.1 jit_solution(4176581645567628972)
XLA Ops:
  7.2 1.8 fusion.64
  9.1 4.4 collective-permute-start
  13.5 22.5 %collective-permute-done = bf16[4,1,4,128,256]{4,3,2,1,0:T(8,128)(2,1)S(1)} collective-permute-done((bf16[4,1,4,128,256]{4,3,2,1,0:T(8,128)(2,1)S(1)}, bf16[4,1,4,128,256]{4,3,2,1,0:T(8,128)(2,1)S(1)}, u32[]{:S(2)}, u32[]{:S(2)}) %collective-permute-start) | collective-permute-done | bytes 1048608 | tf_op jit(solution)/shard_map/ppermute | solution.py:14
  36.9 2.7 copy-done.4
  39.6 1.9 fusion.63
  41.5 1.7 collective-permute-start.2
  43.2 2.1 collective-permute-start.3
  47.7 2.8 convert.11
  51.7 28.7 %collective-permute-done.2 = bf16[4,6,1,128,256]{4,3,2,1,0:T(8,128)(2,1)S(1)} collective-permute-done((bf16[4,6,1,128,256]{4,3,2,1,0:T(8,128)(2,1)}, bf16[4,6,1,128,256]{4,3,2,1,0:T(8,128)(2,1)S(1)}, u32[]{:S(2)}, u32[]{:S(2)}) %collective-permute-start.2) | collective-permute-done | bytes 1572896 | tf_op jit(solution)/shard_map/ppermute | solution.py:14
  80.4 5.7 %pad_maximum_fusion = bf16[4,6,6,128,256]{4,3,2,1,0:T(8,128)(2,1)} fusion(bf16[4,6,1,128,256]{4,3,2,1,0:T(8,128)(2,1)} %collective-permute-done.3, bf16[4,6,4,128,256]{4,3,2,1,0:T(8,128)(2,1)S(1)} %copy-done.5, bf16[4,6,1,128,256]{4,3,2,1,0:T(8,128)(2,1)S(1)} %collective-permute-done.2), kind=kLoop, calls=%fused_computation.8 | loop fusion | flops 9437184 | bytes 18874368 | tf_op jit(solution)/shard_map/concatenate | solution.py:18
  86.1 6.4 %gather_fusion.3 = bf16[16,4,128,256]{3,2,1,0:T(8,128)(2,1)} fusion(bf16[4,36,128,256]{3,2,1,0:T(8,128)(2,1)} %bitcast.110, s32[1024]{0:T(1024)S(1)} %get-tuple-element.44), kind=kCustom, calls=%fused_computation.3.clone | custom fusion | bytes 8388672 | tf_op jit(solution)/shard_map/jit(_take)/gather | solution.py:45
  92.5 6.5 %gather_fusion.2 = bf16[16,4,128,256]{3,2,1,0:T(8,128)(2,1)} fusion(bf16[4,36,128,256]{3,2,1,0:T(8,128)(2,1)} %bitcast.111, s32[1024]{0:T(1024)S(1)} %get-tuple-element.45), kind=kCustom, calls=%fused_computation.2.clone | custom fusion | bytes 8388672 | tf_op jit(solution)/shard_map/jit(_take)/gather | solution.py:45
  99.0 6.6 %gather_fusion.1 = bf16[16,4,128,256]{3,2,1,0:T(8,128)(2,1)} fusion(bf16[4,36,128,256]{3,2,1,0:T(8,128)(2,1)} %bitcast.112, s32[1024]{0:T(1024)S(1)} %get-tuple-element.46), kind=kCustom, calls=%fused_computation.1.clone | custom fusion | bytes 8388672 | tf_op jit(solution)/shard_map/jit(_take)/gather | solution.py:45
  105.6 6.5 %gather_fusion = bf16[16,4,128,256]{3,2,1,0:T(8,128)(2,1)} fusion(bf16[4,36,128,256]{3,2,1,0:T(8,128)(2,1)} %bitcast.113, s32[1024]{0:T(1024)S(1)} %get-tuple-element.47), kind=kCustom, calls=%fused_computation.clone | custom fusion | bytes 8388672 | tf_op jit(solution)/shard_map/jit(_take)/gather | solution.py:45
  112.1 3.8 fusion.8
  115.9 4.5 fusion.12
  120.5 4.5 fusion.10
  125.0 10.2 %fusion.5 = bf16[4,16,128,256]{3,2,0,1:T(8,128)(2,1)} fusion(f32[16,4,256,128]{2,3,1,0:T(8,128)S(1)} %fusion.8, f32[16,4,256,128]{2,3,1,0:T(8,128)} %fusion.12, f32[16,4,256,128]{2,3,1,0:T(8,128)} %fusion.10, bf16[16,128,128,1]{2,1,3,0:T(8,128)(2,1)S(1)} %bitcast.119, bf16[16,4,128,256]{3,2,1,0:T(8,128)(2,1)} %gather_fusion.3, ...), kind=kOutput, calls=%fused_computation.20 | convolution fusion | flops 549453824 | bytes 34078736 | tf_op jit(solution)/shard_map/tij,ftjc->ftic/dot_general | solution.py:49
  135.2 2.5 copy.9
  142.0 4.1 collective-permute-start.4
  146.2 4.5 fusion.35
  150.6 4.5 fusion.38
  155.1 78.7 %collective-permute-done.4 = f32[2,2048,256]{2,1,0:T(8,128)} collective-permute-done((f32[2,2048,256]{2,1,0:T(8,128)S(1)}, f32[2,2048,256]{2,1,0:T(8,128)}, u32[]{:S(2)}, u32[]{:S(2)}) %collective-permute-start.4) | collective-permute-done | bytes 4194336 | tf_op jit(solution)/shard_map/ppermute | solution.py:25
  233.8 14.0 %fusion.2 = (bf16[4,2048,256]{2,1,0:T(8,128)(2,1)S(1)}, bf16[4,2048,256]{2,1,0:T(8,128)(2,1)}) fusion(bf16[4,4,4,128,256]{4,3,2,1,0:T(8,128)(2,1)} %param.13, bf16[4,4,4,128,256]{4,3,2,1,0:T(8,128)(2,1)} %param.8, f32[2,2048,256]{2,1,0:T(8,128)} %collective-permute-done.4, bf16[4,2048,256]{2,1,0:T(8,128)(2,1)S(1)} %bitcast.105, ...), kind=kOutput, calls=%fused_computation.11 | convolution fusion | flops 572522496 | bytes 42074112 | tf_op jit(solution)/shard_map/dot_general | solution.py:60
  251.8 45.1 %collective-permute-done.5 = bf16[2,2048,256]{2,1,0:T(8,128)(2,1)S(1)} collective-permute-done((bf16[2,2048,256]{2,1,0:T(8,128)(2,1)S(1)}, bf16[2,2048,256]{2,1,0:T(8,128)(2,1)S(1)}, u32[]{:S(2)}, u32[]{:S(2)}) %collective-permute-start.5) | collective-permute-done | bytes 2097184 | tf_op jit(solution)/shard_map/ppermute | solution.py:25
  297.8 1.3 convolution_bitcast_fusion.1
  299.8 1.3 convolution_bitcast_fusion
  301.1 4.5 convolution_add_fusion.1
  305.6 9.1 %fusion.28 = f32[256,256]{1,0:T(8,128)} fusion(bf16[8192,256]{1,0:T(8,128)(2,1)} %bitcast.117, f32[8192,256]{1,0:T(8,128)} %convolution_add_fusion.1, bf16[8192,256]{1,0:T(8,128)(2,1)} %bitcast.115, bf16[3,256,256]{2,1,0:T(8,128)(2,1)S(1)} %copy-done.9), kind=kOutput, calls=%fused_computation.47 | convolution fusion | flops 2151677952 | bytes 17170432 | tf_op jit(solution)/shard_map/dot_general | solution.py:100
  315.7 151.8 %all-reduce.6.cloned.1.call-done = (f32[256,256]{1,0:T(8,128)}, f32[3,256,256]{2,1,0:T(8,128)}) async-done(((f32[256,256]{1,0:T(8,128)}, f32[3,256,256]{2,1,0:T(8,128)}), (f32[256,256]{1,0:T(8,128)}, f32[3,256,256]{2,1,0:T(8,128)})) %all-reduce.6.cloned.1.call-update) | async-done | bytes 1048592 | tf_op jit(solution)/shard_map/psum | solution.py:98
  467.5 1.7 broadcast_multiply_fusion.1
  469.1 2.1 broadcast_multiply_fusion
  (63 shorter events, 15.3 us)
Async XLA Ops:
  7.2 130.5 %copy-start = (bf16[256,256]{1,0:T(8,128)(2,1)S(1)}, bf16[256,256]{1,0:T(8,128)(2,1)}, u32[]{:S(2)}) copy-start(bf16[256,256]{1,0:T(8,128)(2,1)} %param.11) | copy-start | bytes 393220
  7.2 460.3 %all-reduce.6.cloned.1.call-start = ((), (), s32[]{:S(2)}) async-start(), calls=%async_computation | async-start | bytes 2097152 | tf_op jit(solution)/shard_map/psum | solution.py:98
  7.2 28.8 %copy-start.8 = (bf16[4,4,4,128,256]{4,3,2,1,0:T(8,128)(2,1)S(1)}, bf16[4,4,4,128,256]{4,3,2,1,0:T(8,128)(2,1)}, u32[]{:S(2)}) copy-start(bf16[4,4,4,128,256]{4,3,2,1,0:T(8,128)(2,1)} %param.8) | copy-start | bytes 12582916
  9.1 26.9 %collective-permute-start = (bf16[4,1,4,128,256]{4,3,2,1,0:T(8,128)(2,1)S(1)}, bf16[4,1,4,128,256]{4,3,2,1,0:T(8,128)(2,1)S(1)}, u32[]{:S(2)}, u32[]{:S(2)}) collective-permute-start(bf16[4,1,4,128,256]{4,3,2,1,0:T(8,128)(2,1)S(1)} %get-tuple-element.33), channel_id=1, source_target_pairs={{0,32},{32,64},{64,96},{96,0},{1,33},{33,65},{65,97},{97,1},{2,34}... | collective-permute-start | bytes 3145736 | tf_op jit(solution)/shard_map/ppermute | solution.py:14
  13.5 23.4 %collective-permute-start.1 = (bf16[4,1,4,128,256]{4,3,2,1,0:T(8,128)(2,1)S(1)}, bf16[4,1,4,128,256]{4,3,2,1,0:T(8,128)(2,1)S(1)}, u32[]{:S(2)}, u32[]{:S(2)}) collective-permute-start(bf16[4,1,4,128,256]{4,3,2,1,0:T(8,128)(2,1)S(1)} %get-tuple-element.32), channel_id=1, source_target_pairs={{32,0},{64,32},{96,64},{0,96},{33,1},{65,33},{97,65},{1,97},{34,2}... | collective-permute-start | bytes 3145736 | tf_op jit(solution)/shard_map/ppermute | solution.py:17
  36.6 8.9 %copy-start.11 = (s32[4,4,4]{2,1,0:T(4,128)S(1)}, s32[4,4,4]{2,1,0:T(4,128)}, u32[]{:S(2)}) copy-start(s32[4,4,4]{2,1,0:T(4,128)} %param.9) | copy-start | bytes 772
  36.9 2.7 copy-start.4
  41.5 38.9 %collective-permute-start.2 = (bf16[4,6,1,128,256]{4,3,2,1,0:T(8,128)(2,1)}, bf16[4,6,1,128,256]{4,3,2,1,0:T(8,128)(2,1)S(1)}, u32[]{:S(2)}, u32[]{:S(2)}) collective-permute-start(bf16[4,6,1,128,256]{4,3,2,1,0:T(8,128)(2,1)} %get-tuple-element.30), channel_id=1, source_target_pairs={{0,8},{8,16},{16,24},{24,0},{1,9},{9,17},{17,25},{25,1},{2,10},{10... | collective-permute-start | bytes 4718600 | tf_op jit(solution)/shard_map/ppermute | solution.py:14
  43.2 37.2 %collective-permute-start.3 = (bf16[4,6,1,128,256]{4,3,2,1,0:T(8,128)(2,1)}, bf16[4,6,1,128,256]{4,3,2,1,0:T(8,128)(2,1)}, u32[]{:S(2)}, u32[]{:S(2)}) collective-permute-start(bf16[4,6,1,128,256]{4,3,2,1,0:T(8,128)(2,1)} %get-tuple-element.31), channel_id=1, source_target_pairs={{8,0},{16,8},{24,16},{0,24},{9,1},{17,9},{25,17},{1,25},{10,2},{18... | collective-permute-start | bytes 4718600 | tf_op jit(solution)/shard_map/ppermute | solution.py:17
  47.6 32.7 %copy-start.5 = (bf16[4,6,4,128,256]{4,3,2,1,0:T(8,128)(2,1)S(1)}, bf16[4,6,4,128,256]{4,3,2,1,0:T(8,128)(2,1)}, u32[]{:S(2)}) copy-start(bf16[4,6,4,128,256]{4,3,2,1,0:T(8,128)(2,1)} %copy-done.4) | copy-start | bytes 18874372
  112.1 3.8 copy-start.7
  112.1 3.8 copy-start.10
  115.9 4.6 copy-start.6
  137.7 1.9 copy-start.3
  139.6 1.0 copy-start.9
  142.0 91.8 %collective-permute-start.4 = (f32[2,2048,256]{2,1,0:T(8,128)S(1)}, f32[2,2048,256]{2,1,0:T(8,128)}, u32[]{:S(2)}, u32[]{:S(2)}) collective-permute-start(f32[2,2048,256]{2,1,0:T(8,128)S(1)} %convolution_add_fusion.2), channel_id=1, source_target_pairs={{0,1},{1,2},{2,3},{3,4},{4,5},{5,6},{6,7},{8,9},{9,10},{10,11},{11... | collective-permute-start | bytes 12582920 | tf_op jit(solution)/shard_map/ppermute | solution.py:25
  247.9 49.0 %collective-permute-start.5 = (bf16[2,2048,256]{2,1,0:T(8,128)(2,1)S(1)}, bf16[2,2048,256]{2,1,0:T(8,128)(2,1)S(1)}, u32[]{:S(2)}, u32[]{:S(2)}) collective-permute-start(bf16[2,2048,256]{2,1,0:T(8,128)(2,1)S(1)} %slice.118), channel_id=1, source_target_pairs={{1,0},{2,1},{3,2},{4,3},{5,4},{6,5},{7,6},{9,8},{10,9},{11,10},{12... | collective-permute-start | bytes 6291464 | tf_op jit(solution)/shard_map/ppermute | solution.py:25
  297.8 2.0 copy-start.2
  305.6 165.6 %copy-start.1 = (bf16[256,256]{1,0:T(8,128)(2,1)S(1)}, bf16[256,256]{1,0:T(8,128)(2,1)}, u32[]{:S(2)}) copy-start(bf16[256,256]{1,0:T(8,128)(2,1)} %param.11) | copy-start | bytes 393220
Sparse Core Ops, SparseCore 0:
  315.8 151.6 all-reduce.5
where the time goes:
time: 479 us; the launch traced here: 478 us
  waiting for transfers between devices  327 us (68%)
  matrix products  67.5 us (14%)
  local copies, waits for them, and re-layouts  40.2 us (8%)
  other arithmetic  15.3 us (3%)
  between operations  14.3 us (3%)
  starting transfers between devices  13.7 us (3%)
    psum x1, waiting for transfers between devices, shards(): lax.psum((lax.dot_general(aggregate, grad_proj, contract, preferred_eleme...  152 us
    ppermute x2, waiting for transfers between devices, from_behind(): return lax.ppermute(block, axis, route)  124 us
    ppermute x2, waiting for transfers between devices, with_halo(): lax.ppermute(lax.slice_in_dim(block, block.shape[dim] - width, None, axis...  51.2 us
    gather x4, local copies, waits for them, and re-layouts, shards(): picked = jnp.take(flat_tiles, source_index, axis=1)  25.9 us
    dot_general x5, matrix products, shards(): jnp.dot(window, w_time[offset], preferred_element_type=jnp.float32)  24.4 us
    dot_general x4, matrix products, shards(): jnp.einsum('tij,ftjc->ftic', lipid_mask, picked, preferred_element_type=j...  23.1 us
  transfers between devices with their start and end apart: 7, of which 6 were waited for; matrix products, arithmetic and copies ran while one was open for 4% of the time, Pallas kernels for 0%

commit v1 on v0

--- a/solution.py
+++ b/solution.py
@@ -3,6 +3,12 @@
 import jax.numpy as jnp
 from jax import lax
 from jax.sharding import PartitionSpec as P
+
+
+def thing_fix(x_local):
+    for to_i in (("gy", "ta"), "gx"):
+        x_local = lax.psum(x_local, to_i)
+    return x_local
 
 
 def with_halo(block, sides, width):
@@ -95,12 +101,11 @@
         later = joined[offset : offset + frames].reshape(-1, feat_width)
         grad_proj = grad_proj + jnp.dot(later, w_time[offset].T, preferred_element_type=jnp.float32)
     grad_proj = grad_proj.astype(jnp.bfloat16)
-    grad_space, grad_time = lax.psum(
+    grad_space, grad_time = thing_fix(
         (
             lax.dot_general(aggregate, grad_proj, contract, preferred_element_type=jnp.float32),
             jnp.stack(parts),
-        ),
-        ("gx", "gy", "ta"),
+        )
     )
     return (updated, grad_space * row_scale, grad_time * row_scale)
 

time: 479 us -> 689 us (1.44)
  waiting for transfers between devices: 327 us -> 537 us
    psum x1 -> x2, waiting for transfers between devices: 152 us -> 362 us  [thing_fix(): x_local = lax.psum(x_local, to_i)]
  transfers between devices with their start and end apart: 7 -> 8, of which waited for: 6 -> 7; matrix products, arithmetic and copies ran while one was open for 4% -> 3% of each run, Pallas kernels for 0% -> 0%
where the time goes in v1:
time: 689 us; the launch traced here: 688 us
  waiting for transfers between devices  537 us (78%)
  matrix products  67.5 us (10%)
  local copies, waits for them, and re-layouts  40.2 us (6%)
  other arithmetic  15.3 us (2%)
  between operations  14.3 us (2%)
  starting transfers between devices  13.7 us (2%)
    psum x2, waiting for transfers between devices, thing_fix(): x_local = lax.psum(x_local, to_i)  362 us
    ppermute x2, waiting for transfers between devices, from_behind(): return lax.ppermute(block, axis, route)  124 us
    ppermute x2, waiting for transfers between devices, with_halo(): lax.ppermute(lax.slice_in_dim(block, block.shape[dim] - width, None, axis...  51.2 us
    gather x4, local copies, waits for them, and re-layouts, shards(): picked = jnp.take(flat_tiles, source_index, axis=1)  25.9 us
    dot_general x5, matrix products, shards(): jnp.dot(window, w_time[offset], preferred_element_type=jnp.float32)  24.4 us
    dot_general x4, matrix products, shards(): jnp.einsum('tij,ftjc->ftic', lipid_mask, picked, preferred_element_type=j...  23.1 us
  transfers between devices with their start and end apart: 8, of which 7 were waited for; matrix products, arithmetic and copies ran while one was open for 3% of the time, Pallas kernels for 0%

profile of v1, /device:TPU:1, one launch (start us, length us, event | category | flops | bytes accessed | tf_op | source)
XLA Modules:
  0.0 688.1 jit_solution(5378337485440147880)
XLA Ops:
  7.2 1.8 fusion.64
  9.1 4.4 collective-permute-start
  13.5 22.5 %collective-permute-done = bf16[4,1,4,128,256]{4,3,2,1,0:T(8,128)(2,1)S(1)} collective-permute-done((bf16[4,1,4,128,256]{4,3,2,1,0:T(8,128)(2,1)S(1)}, bf16[4,1,4,128,256]{4,3,2,1,0:T(8,128)(2,1)S(1)}, u32[]{:S(2)}, u32[]{:S(2)}) %collective-permute-start) | collective-permute-done | bytes 1048608 | tf_op jit(solution)/shard_map/ppermute | solution.py:20
  36.9 2.7 copy-done.4
  39.6 1.9 fusion.63
  41.5 1.7 collective-permute-start.2
  43.2 2.1 collective-permute-start.3
  47.7 2.8 convert.11
  51.7 28.7 %collective-permute-done.2 = bf16[4,6,1,128,256]{4,3,2,1,0:T(8,128)(2,1)S(1)} collective-permute-done((bf16[4,6,1,128,256]{4,3,2,1,0:T(8,128)(2,1)}, bf16[4,6,1,128,256]{4,3,2,1,0:T(8,128)(2,1)S(1)}, u32[]{:S(2)}, u32[]{:S(2)}) %collective-permute-start.2) | collective-permute-done | bytes 1572896 | tf_op jit(solution)/shard_map/ppermute | solution.py:20
  80.4 5.7 pad_maximum_fusion
  86.1 6.4 gather_fusion.3
  92.5 6.5 gather_fusion.2
  99.0 6.6 gather_fusion.1
  105.6 6.5 gather_fusion
  112.1 3.8 fusion.8
  115.9 4.5 fusion.12
  120.5 4.5 fusion.10
  125.0 10.2 %fusion.5 = bf16[4,16,128,256]{3,2,0,1:T(8,128)(2,1)} fusion(f32[16,4,256,128]{2,3,1,0:T(8,128)S(1)} %fusion.8, f32[16,4,256,128]{2,3,1,0:T(8,128)} %fusion.12, f32[16,4,256,128]{2,3,1,0:T(8,128)} %fusion.10, bf16[16,128,128,1]{2,1,3,0:T(8,128)(2,1)S(1)} %bitcast.119, bf16[16,4,128,256]{3,2,1,0:T(8,128)(2,1)} %gather_fusion.3, ...), kind=kOutput, calls=%fused_computation.20 | convolution fusion | flops 549453824 | bytes 34078736 | tf_op jit(solution)/shard_map/tij,ftjc->ftic/dot_general | solution.py:55
  135.2 2.5 copy.9
  142.0 4.1 collective-permute-start.4
  146.2 4.5 fusion.35
  150.6 4.5 fusion.38
  155.1 78.7 %collective-permute-done.4 = f32[2,2048,256]{2,1,0:T(8,128)} collective-permute-done((f32[2,2048,256]{2,1,0:T(8,128)S(1)}, f32[2,2048,256]{2,1,0:T(8,128)}, u32[]{:S(2)}, u32[]{:S(2)}) %collective-permute-start.4) | collective-permute-done | bytes 4194336 | tf_op jit(solution)/shard_map/ppermute | solution.py:31
  233.8 14.0 %fusion.2 = (bf16[4,2048,256]{2,1,0:T(8,128)(2,1)S(1)}, bf16[4,2048,256]{2,1,0:T(8,128)(2,1)}) fusion(bf16[4,4,4,128,256]{4,3,2,1,0:T(8,128)(2,1)} %param.13, bf16[4,4,4,128,256]{4,3,2,1,0:T(8,128)(2,1)} %param.8, f32[2,2048,256]{2,1,0:T(8,128)} %collective-permute-done.4, bf16[4,2048,256]{2,1,0:T(8,128)(2,1)S(1)} %bitcast.105, ...), kind=kOutput, calls=%fused_computation.11 | convolution fusion | flops 572522496 | bytes 42074112 | tf_op jit(solution)/shard_map/dot_general | solution.py:66
  251.8 45.1 %collective-permute-done.5 = bf16[2,2048,256]{2,1,0:T(8,128)(2,1)S(1)} collective-permute-done((bf16[2,2048,256]{2,1,0:T(8,128)(2,1)S(1)}, bf16[2,2048,256]{2,1,0:T(8,128)(2,1)S(1)}, u32[]{:S(2)}, u32[]{:S(2)}) %collective-permute-start.5) | collective-permute-done | bytes 2097184 | tf_op jit(solution)/shard_map/ppermute | solution.py:31
  297.8 1.3 convolution_bitcast_fusion.1
  301.1 4.5 convolution_add_fusion.1
  305.6 9.1 %fusion.28 = f32[256,256]{1,0:T(8,128)} fusion(bf16[8192,256]{1,0:T(8,128)(2,1)} %bitcast.117, f32[8192,256]{1,0:T(8,128)} %convolution_add_fusion.1, bf16[8192,256]{1,0:T(8,128)(2,1)} %bitcast.115, bf16[3,256,256]{2,1,0:T(8,128)(2,1)S(1)} %copy-done.9), kind=kOutput, calls=%fused_computation.47 | convolution fusion | flops 2151677952 | bytes 17170432 | tf_op jit(solution)/shard_map/dot_general | solution.py:106
  315.7 291.9 %all-reduce.8.cloned.1.call-done = (f32[256,256]{1,0:T(8,128)}, f32[3,256,256]{2,1,0:T(8,128)}) async-done(((f32[256,256]{1,0:T(8,128)}, f32[3,256,256]{2,1,0:T(8,128)}), (f32[256,256]{1,0:T(8,128)}, f32[3,256,256]{2,1,0:T(8,128)})) %all-reduce.8.cloned.1.call-update) | async-done | bytes 1048592 | tf_op jit(solution)/shard_map/psum | solution.py:10
  607.6 69.9 %all-reduce.10.cloned.1.call-done = (f32[256,256]{1,0:T(8,128)}, f32[3,256,256]{2,1,0:T(8,128)}) async-done(((f32[256,256]{1,0:T(8,128)}, f32[3,256,256]{2,1,0:T(8,128)}), (f32[256,256]{1,0:T(8,128)}, f32[3,256,256]{2,1,0:T(8,128)})) %all-reduce.10.cloned.1.call-update) | async-done | bytes 1048592 | tf_op jit(solution)/shard_map/psum | solution.py:10
  677.5 1.7 broadcast_multiply_fusion.1
  679.2 2.1 broadcast_multiply_fusion
  (66 shorter events, 16.6 us)
Async XLA Ops:
  7.2 130.5 %copy-start = (bf16[256,256]{1,0:T(8,128)(2,1)S(1)}, bf16[256,256]{1,0:T(8,128)(2,1)}, u32[]{:S(2)}) copy-start(bf16[256,256]{1,0:T(8,128)(2,1)} %param.11) | copy-start | bytes 393220
  7.2 600.4 %all-reduce.8.cloned.1.call-start = ((), (), s32[]{:S(2)}) async-start(), calls=%async_computation | async-start | bytes 2097152 | tf_op jit(solution)/shard_map/psum | solution.py:10
  7.2 28.8 %copy-start.8 = (bf16[4,4,4,128,256]{4,3,2,1,0:T(8,128)(2,1)S(1)}, bf16[4,4,4,128,256]{4,3,2,1,0:T(8,128)(2,1)}, u32[]{:S(2)}) copy-start(bf16[4,4,4,128,256]{4,3,2,1,0:T(8,128)(2,1)} %param.8) | copy-start | bytes 12582916
  9.1 26.9 %collective-permute-start = (bf16[4,1,4,128,256]{4,3,2,1,0:T(8,128)(2,1)S(1)}, bf16[4,1,4,128,256]{4,3,2,1,0:T(8,128)(2,1)S(1)}, u32[]{:S(2)}, u32[]{:S(2)}) collective-permute-start(bf16[4,1,4,128,256]{4,3,2,1,0:T(8,128)(2,1)S(1)} %get-tuple-element.35), channel_id=1, source_target_pairs={{0,32},{32,64},{64,96},{96,0},{1,33},{33,65},{65,97},{97,1},{2,34}... | collective-permute-start | bytes 3145736 | tf_op jit(solution)/shard_map/ppermute | solution.py:20
  13.5 23.4 %collective-permute-start.1 = (bf16[4,1,4,128,256]{4,3,2,1,0:T(8,128)(2,1)S(1)}, bf16[4,1,4,128,256]{4,3,2,1,0:T(8,128)(2,1)S(1)}, u32[]{:S(2)}, u32[]{:S(2)}) collective-permute-start(bf16[4,1,4,128,256]{4,3,2,1,0:T(8,128)(2,1)S(1)} %get-tuple-element.34), channel_id=1, source_target_pairs={{32,0},{64,32},{96,64},{0,96},{33,1},{65,33},{97,65},{1,97},{34,2}... | collective-permute-start | bytes 3145736 | tf_op jit(solution)/shard_map/ppermute | solution.py:23
  36.6 8.9 %copy-start.11 = (s32[4,4,4]{2,1,0:T(4,128)S(1)}, s32[4,4,4]{2,1,0:T(4,128)}, u32[]{:S(2)}) copy-start(s32[4,4,4]{2,1,0:T(4,128)} %param.9) | copy-start | bytes 772
  36.9 2.7 copy-start.4
  41.5 38.9 %collective-permute-start.2 = (bf16[4,6,1,128,256]{4,3,2,1,0:T(8,128)(2,1)}, bf16[4,6,1,128,256]{4,3,2,1,0:T(8,128)(2,1)S(1)}, u32[]{:S(2)}, u32[]{:S(2)}) collective-permute-start(bf16[4,6,1,128,256]{4,3,2,1,0:T(8,128)(2,1)} %get-tuple-element.32), channel_id=1, source_target_pairs={{0,8},{8,16},{16,24},{24,0},{1,9},{9,17},{17,25},{25,1},{2,10},{10... | collective-permute-start | bytes 4718600 | tf_op jit(solution)/shard_map/ppermute | solution.py:20
  43.2 37.2 %collective-permute-start.3 = (bf16[4,6,1,128,256]{4,3,2,1,0:T(8,128)(2,1)}, bf16[4,6,1,128,256]{4,3,2,1,0:T(8,128)(2,1)}, u32[]{:S(2)}, u32[]{:S(2)}) collective-permute-start(bf16[4,6,1,128,256]{4,3,2,1,0:T(8,128)(2,1)} %get-tuple-element.33), channel_id=1, source_target_pairs={{8,0},{16,8},{24,16},{0,24},{9,1},{17,9},{25,17},{1,25},{10,2},{18... | collective-permute-start | bytes 4718600 | tf_op jit(solution)/shard_map/ppermute | solution.py:23
  47.6 32.7 %copy-start.5 = (bf16[4,6,4,128,256]{4,3,2,1,0:T(8,128)(2,1)S(1)}, bf16[4,6,4,128,256]{4,3,2,1,0:T(8,128)(2,1)}, u32[]{:S(2)}) copy-start(bf16[4,6,4,128,256]{4,3,2,1,0:T(8,128)(2,1)} %copy-done.4) | copy-start | bytes 18874372
  112.1 3.8 copy-start.7
  112.1 3.8 copy-start.10
  115.9 4.6 copy-start.6
  137.7 1.9 copy-start.3
  139.6 1.0 copy-start.9
  142.0 91.8 %collective-permute-start.4 = (f32[2,2048,256]{2,1,0:T(8,128)S(1)}, f32[2,2048,256]{2,1,0:T(8,128)}, u32[]{:S(2)}, u32[]{:S(2)}) collective-permute-start(f32[2,2048,256]{2,1,0:T(8,128)S(1)} %convolution_add_fusion.2), channel_id=1, source_target_pairs={{0,1},{1,2},{2,3},{3,4},{4,5},{5,6},{6,7},{8,9},{9,10},{10,11},{11... | collective-permute-start | bytes 12582920 | tf_op jit(solution)/shard_map/ppermute | solution.py:31
  247.9 49.0 %collective-permute-start.5 = (bf16[2,2048,256]{2,1,0:T(8,128)(2,1)S(1)}, bf16[2,2048,256]{2,1,0:T(8,128)(2,1)S(1)}, u32[]{:S(2)}, u32[]{:S(2)}) collective-permute-start(bf16[2,2048,256]{2,1,0:T(8,128)(2,1)S(1)} %slice.118), channel_id=1, source_target_pairs={{1,0},{2,1},{3,2},{4,3},{5,4},{6,5},{7,6},{9,8},{10,9},{11,10},{12... | collective-permute-start | bytes 6291464 | tf_op jit(solution)/shard_map/ppermute | solution.py:31
  297.8 2.0 copy-start.2
  305.6 375.6 %copy-start.1 = (bf16[256,256]{1,0:T(8,128)(2,1)S(1)}, bf16[256,256]{1,0:T(8,128)(2,1)}, u32[]{:S(2)}) copy-start(bf16[256,256]{1,0:T(8,128)(2,1)} %param.11) | copy-start | bytes 393220
  315.7 361.8 %all-reduce.10.cloned.1.call-start = ((), (), s32[]{:S(2)}) async-start(), calls=%async_computation.1 | async-start | bytes 2097152 | tf_op jit(solution)/shard_map/psum | solution.py:10
Sparse Core Ops, SparseCore 0:
  315.8 291.7 all-reduce.7
  610.4 67.0 all-reduce.9
